TPU v7x, 128 devices: a whole 4x4x4 slice. The times are simulated.
128 devices in a mesh: dp: 16 (over y, x), fsdp: 8 (over z, core).
Axes of the slice: x: 4, y: 4, z: 4, core: 2. Of those that a mesh axis runs over, the one named last changes fastest.
Arguments:
- block_input: bfloat16 [2, 16384, 1024], P(None, ('dp', 'fsdp')), may hold values from -6 to 6
- seq_start: int32 [2, 16384], P(None, ('dp', 'fsdp')), may hold values from 0 to 15871, as said below
- norm_gain: bfloat16 [1024], P('fsdp'), may hold values from 0.099609375 to 1.8984375
- in_weight: bfloat16 [1024, 3072], P('fsdp'), may hold values from -0.1875 to 0.1875
- conv_weight: bfloat16 [3, 1024], P(None, 'fsdp'), may hold values from -3.5 to 3.5
- out_weight: bfloat16 [1024, 1024], P('fsdp'), may hold values from -0.1875 to 0.1875
- ffn_gain: bfloat16 [1024], P('fsdp'), may hold values from 0.099609375 to 1.8984375
- gate_weight: bfloat16 [1024, 4608], P('fsdp'), may hold values from -0.1875 to 0.1875
- up_weight: bfloat16 [1024, 4608], P('fsdp'), may hold values from -0.1875 to 0.1875
- down_weight: bfloat16 [4608, 1024], P('fsdp'), may hold values from -0.125 to 0.125
- cotangent: bfloat16 [2, 16384, 1024], P(None, ('dp', 'fsdp')), may hold values from -24 to 24
Outputs:
- block_output: bfloat16 [2, 16384, 1024], P(None, ('dp', 'fsdp'))
- input_grad: float32 [2, 16384, 1024], P(None, ('dp', 'fsdp'))
- norm_gain_grad: float32 [1024], P('fsdp')
- in_weight_grad: float32 [1024, 3072], P('fsdp')
- conv_weight_grad: float32 [3, 1024], P(None, 'fsdp')
- out_weight_grad: float32 [1024, 1024], P('fsdp')
- ffn_gain_grad: float32 [1024], P('fsdp')
- gate_weight_grad: float32 [1024, 4608], P('fsdp')
- up_weight_grad: float32 [1024, 4608], P('fsdp')
- down_weight_grad: float32 [4608, 1024], P('fsdp')
Inputs may be any that keep to these rules, and one draw needn't show every extreme that they name: seq_start is the index within the micro-batch of the first token of the token's sequence; it never falls along a micro-batch, the first sequence starts at 0, and every sequence holds between 512 and 1536 tokens.
All inputs are finite; a program needn't handle non-finite values.
Results may differ from a plain program's by a relative error of at most 0.018.
Values may be sent and summed in bfloat16 or wider, within the bound.
No kernel may reach another device: no remote copies, remote signals or barrier semaphores. Data moves between devices by JAX's collectives and lax.ppermute only.
A program may use at most 256 MiB of HBM per device.

v0:
```python
import jax
import jax.numpy as jnp
from jax import lax
from jax.sharding import PartitionSpec as P

KW = 3


EPS = 1e-05
CONTRACT = (((0,), (0,)), ((), ()))
BACK_DIMS = (((1,), (1,)), ((), ()))


def from_behind(block, axis, distance):
    devices = range(lax.axis_size(axis))
    route = [(i - distance, i) for i in devices if i - distance in devices]
    return lax.ppermute(block, axis, route)


def reorder(value, axis, outer, inner):
    shape = value.shape
    piece = shape[axis] // (outer * inner)
    split = value.reshape(shape[:axis] + (outer, inner, piece) + shape[axis + 1 :])
    return jnp.swapaxes(split, axis, axis + 1).reshape(shape)


def forward(inputs, starts, position, weights):
    norm_gain, in_weight, conv_weight, out_weight, ffn_gain, gate_weight, up_weight, down_weight = (
        weights
    )
    model_width = inputs.shape[1]
    tok_rows = inputs.shape[0]
    inv_one = lax.rsqrt(jnp.mean(inputs * inputs, -1, keepdims=True) + EPS)
    normed_one = (inputs * inv_one * norm_gain.astype(jnp.float32)).astype(jnp.bfloat16)
    projected = jnp.dot(normed_one, in_weight, preferred_element_type=jnp.float32)
    b_part = projected[:, :model_width]
    c_part = projected[:, model_width : 2 * model_width]
    x_part = projected[:, 2 * model_width :]
    mixed = b_part * x_part
    rim_rows = from_behind(mixed[tok_rows - (KW - 1) :], ("dp", "fsdp"), 1)
    extended = jnp.concatenate([rim_rows, mixed], 0)
    conv_taps = conv_weight.astype(jnp.float32)
    tap_masks = [
        (position - tap_index >= starts).astype(jnp.float32)[:, None] for tap_index in range(KW)
    ]
    conv_out = jnp.zeros_like(mixed)
    for tap_index in range(KW):
        lower = KW - 1 - tap_index
        conv_out = (
            conv_out
            + conv_taps[tap_index] * extended[lower : lower + tok_rows] * tap_masks[tap_index]
        )
    gated = (c_part * conv_out).astype(jnp.bfloat16)
    resid = inputs + jnp.dot(gated, out_weight, preferred_element_type=jnp.float32)
    inv_two = lax.rsqrt(jnp.mean(resid * resid, -1, keepdims=True) + EPS)
    normed_two = (resid * inv_two * ffn_gain.astype(jnp.float32)).astype(jnp.bfloat16)
    gate_pre = jnp.dot(normed_two, gate_weight, preferred_element_type=jnp.float32)
    up_pre = jnp.dot(normed_two, up_weight, preferred_element_type=jnp.float32)
    hidden = (jax.nn.silu(gate_pre) * up_pre).astype(jnp.bfloat16)
    result = (resid + jnp.dot(hidden, down_weight, preferred_element_type=jnp.float32)).astype(
        jnp.bfloat16
    )
    kept_values = (
        inv_one,
        normed_one,
        b_part,
        c_part,
        x_part,
        extended,
        tap_masks,
        conv_out,
        gated,
        resid,
        inv_two,
        normed_two,
        gate_pre,
        up_pre,
        hidden,
    )
    return (result, kept_values)


def backward(inputs, grad_out, kept_values, weights, arrange):
    (
        inv_one,
        normed_one,
        b_part,
        c_part,
        x_part,
        extended,
        tap_masks,
        conv_out,
        gated,
        resid,
        inv_two,
        normed_two,
        gate_pre,
        up_pre,
        hidden,
    ) = kept_values
    norm_gain, in_weight, conv_weight, out_weight, ffn_gain, gate_weight, up_weight, down_weight = (
        weights
    )
    tok_rows = inputs.shape[0]
    grad_low = grad_out.astype(jnp.bfloat16)
    down_term = lax.dot_general(
        arrange(hidden, 1), grad_low, CONTRACT, preferred_element_type=jnp.float32
    )
    grad_hidden = lax.dot_general(
        grad_low, down_weight, BACK_DIMS, preferred_element_type=jnp.float32
    )
    sigma = jax.nn.sigmoid(gate_pre)
    grad_gate = (grad_hidden * up_pre * sigma * (1.0 + gate_pre * (1.0 - sigma))).astype(
        jnp.bfloat16
    )
    grad_up = (grad_hidden * gate_pre * sigma).astype(jnp.bfloat16)
    normed_moved = arrange(normed_two, 1)
    gate_term = lax.dot_general(
        normed_moved, grad_gate, CONTRACT, preferred_element_type=jnp.float32
    )
    up_term = lax.dot_general(normed_moved, grad_up, CONTRACT, preferred_element_type=jnp.float32)
    grad_normed = lax.dot_general(
        grad_gate, gate_weight, BACK_DIMS, preferred_element_type=jnp.float32
    )
    grad_normed = grad_normed + lax.dot_general(
        grad_up, up_weight, BACK_DIMS, preferred_element_type=jnp.float32
    )
    ffn_term = arrange(jnp.sum(grad_normed * resid * inv_two, 0), 0)
    hat_two = grad_normed * ffn_gain.astype(jnp.float32)
    grad_resid = (
        grad_out
        + inv_two * hat_two
        - resid * inv_two**3 * jnp.mean(hat_two * resid, -1, keepdims=True)
    )
    grad_branch = grad_resid.astype(jnp.bfloat16)
    out_term = lax.dot_general(
        arrange(gated, 1), grad_branch, CONTRACT, preferred_element_type=jnp.float32
    )
    grad_gated = lax.dot_general(
        grad_branch, out_weight, BACK_DIMS, preferred_element_type=jnp.float32
    )
    grad_c = grad_gated * conv_out
    grad_conv = grad_gated * c_part
    conv_taps = conv_weight.astype(jnp.float32)
    tap_terms = []
    grad_extended = jnp.zeros_like(extended)
    for tap_index in range(KW):
        lower = KW - 1 - tap_index
        masked = grad_conv * tap_masks[tap_index]
        tap_terms.append(arrange(jnp.sum(masked * extended[lower : lower + tok_rows], 0), 0))
        grad_extended = grad_extended + jnp.pad(
            masked * conv_taps[tap_index], ((lower, tap_index), (0, 0))
        )
    conv_term = jnp.stack(tap_terms, 0)
    incoming = from_behind(grad_extended[: KW - 1], ("dp", "fsdp"), -1)
    grad_mixed = grad_extended[KW - 1 :] + jnp.pad(incoming, ((tok_rows - (KW - 1), 0), (0, 0)))
    grad_projected = jnp.concatenate([grad_mixed * x_part, grad_c, grad_mixed * b_part], 1).astype(
        jnp.bfloat16
    )
    in_term = lax.dot_general(
        arrange(normed_one, 1), grad_projected, CONTRACT, preferred_element_type=jnp.float32
    )
    grad_first = lax.dot_general(
        grad_projected, in_weight, BACK_DIMS, preferred_element_type=jnp.float32
    )
    norm_term = arrange(jnp.sum(grad_first * inputs * inv_one, 0), 0)
    hat_one = grad_first * norm_gain.astype(jnp.float32)
    grad_input = (
        grad_resid
        + inv_one * hat_one
        - inputs * inv_one**3 * jnp.mean(hat_one * inputs, -1, keepdims=True)
    )
    terms = (norm_term, in_term, conv_term, out_term, ffn_term, gate_term, up_term, down_term)
    return (terms, grad_input)


def shards(
    block_input,
    seq_start,
    norm_gain,
    in_weight,
    conv_weight,
    out_weight,
    ffn_gain,
    gate_weight,
    up_weight,
    down_weight,
    cotangent,
):
    micro_count, tok_rows, model_width = block_input.shape
    n_fsdp = lax.axis_size("fsdp")
    n_data = lax.axis_size("dp")

    def arrange(value, axis):
        return reorder(value, axis, n_fsdp, n_data)

    position = lax.axis_index(("dp", "fsdp")) * tok_rows + lax.iota(jnp.int32, tok_rows)
    params = (
        norm_gain,
        in_weight,
        conv_weight,
        out_weight,
        ffn_gain,
        gate_weight,
        up_weight,
        down_weight,
    )
    outputs = []
    input_grads = []
    totals = None
    for micro_step in range(micro_count):
        inputs = block_input[micro_step].astype(jnp.float32)
        weights = (
            lax.all_gather(params[0], "fsdp", axis=0, tiled=True),
            lax.all_gather(params[1], "fsdp", axis=0, tiled=True),
            lax.all_gather(params[2], "fsdp", axis=1, tiled=True),
            lax.all_gather(params[3], "fsdp", axis=0, tiled=True),
            lax.all_gather(params[4], "fsdp", axis=0, tiled=True),
            lax.all_gather(params[5], "fsdp", axis=0, tiled=True),
            lax.all_gather(params[6], "fsdp", axis=0, tiled=True),
            lax.all_gather(params[7], "fsdp", axis=0, tiled=True),
        )
        result, kept_values = forward(inputs, seq_start[micro_step], position, weights)
        terms, grad_input = backward(
            inputs, cotangent[micro_step].astype(jnp.float32), kept_values, weights, arrange
        )
        totals = terms if totals is None else tuple((a + b for a, b in zip(totals, terms)))
        outputs.append(result)
        input_grads.append(grad_input)
    shares = (
        lax.psum_scatter(totals[0], ("dp", "fsdp"), scatter_dimension=0, tiled=True),
        lax.psum_scatter(totals[1], ("dp", "fsdp"), scatter_dimension=0, tiled=True),
        lax.psum_scatter(totals[2], ("dp", "fsdp"), scatter_dimension=1, tiled=True),
        lax.psum_scatter(totals[3], ("dp", "fsdp"), scatter_dimension=0, tiled=True),
        lax.psum_scatter(totals[4], ("dp", "fsdp"), scatter_dimension=0, tiled=True),
        lax.psum_scatter(totals[5], ("dp", "fsdp"), scatter_dimension=0, tiled=True),
        lax.psum_scatter(totals[6], ("dp", "fsdp"), scatter_dimension=0, tiled=True),
        lax.psum_scatter(totals[7], ("dp", "fsdp"), scatter_dimension=0, tiled=True),
    )
    finals = (
        lax.all_gather(shares[0].astype(jnp.bfloat16), "dp", axis=0, tiled=True).astype(
            jnp.float32
        ),
        lax.all_gather(shares[1].astype(jnp.bfloat16), "dp", axis=0, tiled=True).astype(
            jnp.float32
        ),
        lax.all_gather(shares[2].astype(jnp.bfloat16), "dp", axis=1, tiled=True).astype(
            jnp.float32
        ),
        lax.all_gather(shares[3].astype(jnp.bfloat16), "dp", axis=0, tiled=True).astype(
            jnp.float32
        ),
        lax.all_gather(shares[4].astype(jnp.bfloat16), "dp", axis=0, tiled=True).astype(
            jnp.float32
        ),
        lax.all_gather(shares[5].astype(jnp.bfloat16), "dp", axis=0, tiled=True).astype(
            jnp.float32
        ),
        lax.all_gather(shares[6].astype(jnp.bfloat16), "dp", axis=0, tiled=True).astype(
            jnp.float32
        ),
        lax.all_gather(shares[7].astype(jnp.bfloat16), "dp", axis=0, tiled=True).astype(
            jnp.float32
        ),
    )
    return (
        jnp.stack(outputs, 0),
        jnp.stack(input_grads, 0),
        finals[0],
        finals[1],
        finals[2],
        finals[3],
        finals[4],
        finals[5],
        finals[6],
        finals[7],
    )


def solution(mesh):
    return jax.shard_map(
        shards,
        mesh=mesh,
        in_specs=(
            P(None, ("dp", "fsdp"), None),
            P(None, ("dp", "fsdp")),
            P("fsdp"),
            P("fsdp", None),
            P(None, "fsdp"),
            P("fsdp", None),
            P("fsdp"),
            P("fsdp", None),
            P("fsdp", None),
            P("fsdp", None),
            P(None, ("dp", "fsdp"), None),
        ),
        out_specs=(
            P(None, ("dp", "fsdp"), None),
            P(None, ("dp", "fsdp"), None),
            P("fsdp"),
            P("fsdp", None),
            P(None, "fsdp"),
            P("fsdp", None),
            P("fsdp"),
            P("fsdp", None),
            P("fsdp", None),
            P("fsdp", None),
        ),
        check_vma=False,
    )
```

profile of v0, /device:TPU:0, one launch (start us, length us, event | category | flops | bytes accessed | tf_op | source)
XLA Modules:
  0.0 1847.5 jit_solution(2323969845612677173)
XLA Ops:
  10.7 11.9 all-gather
  22.6 8.1 all-gather.1
  30.6 9.5 all_gather.58
  41.6 11.8 all-gather.13.cloned.1.call-done
  53.4 4.0 fusion.32
  65.5 15.0 all-gather.15.cloned.1.call-done
  80.5 3.0 multiply_reduce_fusion.10
  86.7 50.2 %all-gather.17.cloned.1.call-done = bf16[1024,4608]{1,0:T(8,128)(2,1)} async-done(((bf16[128,4608]{1,0:T(8,128)(2,1)}), bf16[1024,4608]{1,0:T(8,128)(2,1)}) %all-gather.17.cloned.1.call-update) | async-done | bytes 9437200 | tf_op jit(solution)/shard_map/all_gather | solution.py:219
  136.9 6.5 fusion.68
  143.4 49.5 %all-gather.19.cloned.1.call-done = bf16[1024,4608]{1,0:T(8,128)(2,1)} async-done(((bf16[128,4608]{1,0:T(8,128)(2,1)}), bf16[1024,4608]{1,0:T(8,128)(2,1)}) %all-gather.19.cloned.1.call-update) | async-done | bytes 9437200 | tf_op jit(solution)/shard_map/all_gather | solution.py:220
  192.9 6.5 fusion.69
  199.4 49.5 %all-gather.21.cloned.1.call-done = bf16[4608,1024]{1,0:T(8,128)(2,1)} async-done(((bf16[576,1024]{1,0:T(8,128)(2,1)}), bf16[4608,1024]{1,0:T(8,128)(2,1)}) %all-gather.21.cloned.1.call-update) | async-done | bytes 9437200 | tf_op jit(solution)/shard_map/all_gather | solution.py:221
  248.9 10.4 multiply_convert_fusion.2
  259.3 10.3 fusion.74
  269.6 3.9 fusion.72
  273.5 5.0 multiply_reduce_fusion.1
  280.4 5.2 fusion.70
  285.7 6.6 fusion.71
  292.3 6.3 multiply_convert_fusion
  299.7 12.0 convolution_add_fusion.2
  312.1 10.6 fusion.75
  322.6 13.0 convolution_add_fusion.1
  338.1 3.0 reshape.264
  349.1 3.0 reshape.266
  354.7 3.0 reshape.267
  357.7 10.8 fusion.37
  368.5 12.9 convolution_add_fusion
  381.4 382.3 %fusion = f32[40,1024]{1,0:T(8,128)} fusion(f32[4608,1024]{1,0:T(8,128)} %convolution_add_fusion), kind=kCustom, calls=%all-reduce-scatter | all-reduce-scatter fusion | flops 5242881 | bytes 19038208
  779.2 8.0 collective-permute-start.9
  799.6 3.1 collective-permute-start.5
  802.7 3.7 collective-permute-start.4
  806.4 8.0 fusion.73
  814.5 21.1 %concatenate.18 = bf16[548,1024]{1,0:T(8,128)(2,1)} concatenate(bf16[28,1024]{1,0:T(8,128)(2,1)} %copy-done.60, bf16[40,1024]{1,0:T(8,128)(2,1)S(1)} %collective-permute-done.15, bf16[40,1024]{1,0:T(8,128)(2,1)} %collective-permute-done.14, bf16[40,1024]{1,0:T(8,128)(2,1)} %collective-permute-done.13, bf16[40,1024]{1,0:T(8,128)(2,1)} %collective-permute-done.12, ...), dimensions={0} | concatenate | bytes 2326528
  837.2 7.5 multiply_reduce_fusion
  867.8 6.3 convolution_add_fusion.3
  878.7 5.6 fusion.3
  884.4 5.1 fusion.4
  892.0 5.1 fusion.25
  897.2 6.1 fusion.24
  903.5 76.8 %all-reduce.15 = (bf16[1024]{0:T(1024)(128)(2,1)S(1)}, bf16[3,1024]{1,0:T(4,128)(2,1)S(1)}, bf16[1024]{0:T(1024)(128)(2,1)S(1)}) all-reduce(f32[1024]{0:T(1024)S(1)} %add.271, f32[3,1024]{1,0:T(4,128)S(1)} %maximum_add_fusion, f32[1024]{0:T(1024)S(1)} %add.278), channel_id=2, replica_groups=mesh['dp'=16,'fsdp'=8] {'dp','fsdp'}, use_global_device_ids=true, to_apply=%region_10.11.clone | all-reduce | flops 5120 | bytes 30720
  980.9 37.5 %all-reduce.16 = (bf16[128]{0:T(256)(128)(2,1)S(1)}, bf16[128]{0:T(256)(128)(2,1)S(1)}) all-reduce(bf16[128]{0:T(256)(128)(2,1)S(1)} %dynamic-update-slice, bf16[128]{0:T(256)(128)(2,1)S(1)} %dynamic-update-slice.1), channel_id=1, replica_groups=mesh['dp'=16,'fsdp'=8] {'dp'}, use_global_device_ids=true, to_apply=%add.8 | all-reduce | flops 256 | bytes 1024
  1018.9 20.2 %all-gather.2 = bf16[16,8,3]{1,2,0:T(4,128)(2,1)S(1)} all-gather(bf16[1,8,3]{1,2,0:T(4,128)(2,1)S(1)} %fusion.59), channel_id=1, replica_groups=mesh['dp'=16,'fsdp'=8] {'dp'}, dimensions={0}, use_global_device_ids=true | all-gather | bytes 816 | tf_op jit(solution)/shard_map/all_gather | solution.py:247
  1045.7 483.1 %reduce-scatter.10.cloned.1.call-done = f32[8,1024]{1,0:T(8,128)} async-done(((f32[1024,1024]{1,0:T(8,128)}), f32[8,1024]{1,0:T(8,128)}) %reduce-scatter.10.cloned.1.call-update) | async-done | bytes 32784 | tf_op jit(solution)/shard_map/reduce_scatter | solution.py:234
  1529.6 20.7 %all_gather.67 = bf16[128,1024]{1,0:T(8,128)(2,1)S(1)} all-gather(bf16[8,1024]{1,0:T(8,128)(2,1)S(1)} %convert_element_type.251), channel_id=1, replica_groups=mesh['dp'=16,'fsdp'=8] {'dp'}, dimensions={0}, use_global_device_ids=true | all-gather | bytes 278528 | tf_op jit(solution)/shard_map/all_gather | solution.py:250
  1551.1 198.7 %reduce-scatter.8.cloned.1.call-done = f32[8,3072]{1,0:T(8,128)} async-done(((f32[1024,3072]{1,0:T(8,128)}), f32[8,3072]{1,0:T(8,128)}) %reduce-scatter.8.cloned.1.call-update) | async-done | bytes 98320 | tf_op jit(solution)/shard_map/reduce_scatter | solution.py:232
  1750.7 22.8 %all_gather.65 = bf16[128,3072]{1,0:T(8,128)(2,1)S(1)} all-gather(bf16[8,3072]{1,0:T(8,128)(2,1)S(1)} %convert_element_type.247), channel_id=1, replica_groups=mesh['dp'=16,'fsdp'=8] {'dp'}, dimensions={0}, use_global_device_ids=true | all-gather | bytes 835584 | tf_op jit(solution)/shard_map/all_gather | solution.py:244
  1774.8 17.8 all-gather.23.cloned.1.call-done
  1795.6 41.7 %all-gather.25.cloned.1.call-done = bf16[128,4608]{1,0:T(8,128)(2,1)} async-done(((bf16[8,4608]{1,0:T(8,128)(2,1)}), bf16[128,4608]{1,0:T(8,128)(2,1)}) %all-gather.25.cloned.1.call-update) | async-done | bytes 1179664 | tf_op jit(solution)/shard_map/all_gather | solution.py:259
  (371 shorter events, 107.7 us)
Async XLA Ops:
  7.2 23.4 %copy-start.83 = (bf16[3,128]{1,0:T(4,128)(2,1)S(1)}, bf16[3,128]{1,0:T(4,128)(2,1)}, u32[]{:S(2)}) copy-start(bf16[3,128]{1,0:T(4,128)(2,1)} %param.15) | copy-start | bytes 2308
  7.2 32.9 %copy-start.2 = (bf16[2,128,1024]{2,1,0:T(8,128)(2,1)S(1)}, bf16[2,128,1024]{2,1,0:T(8,128)(2,1)}, u32[]{:S(2)}) copy-start(bf16[2,128,1024]{2,1,0:T(8,128)(2,1)} %param.11) | copy-start | bytes 1572868
  7.2 46.2 %all-gather.13.cloned.1.call-start = ((), (), s32[]{:S(2)}) async-start(), calls=%async_computation.4 | async-start | bytes 7077888 | tf_op jit(solution)/shard_map/all_gather | solution.py:215
  8.0 33.5 %copy-start.84 = (s32[2,128]{1,0:T(2,128)S(1)}, s32[2,128]{1,0:T(2,128)}, u32[]{:S(2)}) copy-start(s32[2,128]{1,0:T(2,128)} %param.12) | copy-start | bytes 3076
  8.0 72.5 %all-gather.15.cloned.1.call-start = ((), (), s32[]{:S(2)}) async-start(), calls=%async_computation.5 | async-start | bytes 2359296 | tf_op jit(solution)/shard_map/all_gather | solution.py:217
  8.7 128.2 %all-gather.17.cloned.1.call-start = ((), (), s32[]{:S(2)}) async-start(), calls=%async_computation.6 | async-start | bytes 10616832 | tf_op jit(solution)/shard_map/all_gather | solution.py:219
  9.4 183.4 %all-gather.19.cloned.1.call-start = ((), (), s32[]{:S(2)}) async-start(), calls=%async_computation.7 | async-start | bytes 10616832 | tf_op jit(solution)/shard_map/all_gather | solution.py:220
  10.0 238.9 %all-gather.21.cloned.1.call-start = ((), (), s32[]{:S(2)}) async-start(), calls=%async_computation.8 | async-start | bytes 10616832 | tf_op jit(solution)/shard_map/all_gather | solution.py:221
  10.6 863.6 %reduce-scatter.12.cloned.1.call-start = ((), (), s32[]{:S(2)}) async-start(), calls=%async_computation.11 | async-start | bytes 19021824 | tf_op jit(solution)/shard_map/reduce_scatter | solution.py:236
  22.5 34.9 %copy-start.61 = (bf16[8,1,128]{2,1,0:T(2,128)(2,1)}, bf16[8,1,128]{2,1,0:T(2,128)(2,1)S(1)}, u32[]{:S(2)}) copy-start(bf16[8,1,128]{2,1,0:T(2,128)(2,1)S(1)} %all-gather) | copy-start | bytes 6148
  22.5 37.2 %copy-start.52 = (f32[8,1,128]{2,1,0:T(1,128)}, f32[8,1,128]{2,1,0:T(1,128)S(1)}, u32[]{:S(2)}) copy-start(f32[8,1,128]{2,1,0:T(1,128)S(1)} %convert_element_type.265) | copy-start | bytes 12292
  41.5 21.7 %copy-start.69 = (f32[128]{0:T(128)}, f32[128]{0:T(128)S(1)}, u32[]{:S(2)}) copy-start(f32[128]{0:T(128)S(1)} %get-tuple-element.85) | copy-start | bytes 1540
  41.5 21.7 %copy-start.75 = (f32[128]{0:T(128)}, f32[128]{0:T(128)S(1)}, u32[]{:S(2)}) copy-start(f32[128]{0:T(128)S(1)} %get-tuple-element.88) | copy-start | bytes 1540
  41.5 22.8 %copy-start.67 = (f32[128]{0:T(128)}, f32[128]{0:T(128)S(1)}, u32[]{:S(2)}) copy-start(f32[128]{0:T(128)S(1)} %get-tuple-element.84) | copy-start | bytes 1540
  41.5 22.8 %copy-start.71 = (f32[128]{0:T(128)}, f32[128]{0:T(128)S(1)}, u32[]{:S(2)}) copy-start(f32[128]{0:T(128)S(1)} %get-tuple-element.86) | copy-start | bytes 1540
  41.5 22.8 %copy-start.73 = (f32[128]{0:T(128)}, f32[128]{0:T(128)S(1)}, u32[]{:S(2)}) copy-start(f32[128]{0:T(128)S(1)} %get-tuple-element.87) | copy-start | bytes 1540
  41.6 22.8 %copy-start.54 = (f32[1,1024]{1,0:T(1,128)}, f32[1,1024]{1,0:T(1,128)S(1)}, u32[]{:S(2)}) copy-start(f32[1,1024]{1,0:T(1,128)S(1)} %get-tuple-element.80) | copy-start | bytes 12292
  41.6 22.8 %copy-start.56 = (f32[1,1024]{1,0:T(1,128)}, f32[1,1024]{1,0:T(1,128)S(1)}, u32[]{:S(2)}) copy-start(f32[1,1024]{1,0:T(1,128)S(1)} %get-tuple-element.81) | copy-start | bytes 12292
  41.6 22.8 %copy-start.58 = (f32[1,1024]{1,0:T(1,128)}, f32[1,1024]{1,0:T(1,128)S(1)}, u32[]{:S(2)}) copy-start(f32[1,1024]{1,0:T(1,128)S(1)} %get-tuple-element.82) | copy-start | bytes 12292
  57.5 5.6 collective-permute-start.1
  60.9 3.4 collective-permute-start
  199.4 59.9 %copy-start.28 = (bf16[128,16,8,8]{0,3,2,1:T(8,128)(2,1)S(1)}, bf16[128,16,8,8]{0,3,2,1:T(8,128)(2,1)}, u32[]{:S(2)}) copy-start(bf16[128,16,8,8]{0,3,2,1:T(8,128)(2,1)} %copy.90) | copy-start | bytes 786436
  311.8 578.5 %reduce-scatter.14.cloned.1.call-start = ((), (), s32[]{:S(2)}) async-start(), calls=%async_computation.13 | async-start | bytes 19021824 | tf_op jit(solution)/shard_map/reduce_scatter | solution.py:237
  335.6 707.5 %all-gather.27.cloned.1.call-start = ((), (), s32[]{:S(2)}) async-start(), calls=%async_computation.15 | async-start | bytes 1392640 | tf_op jit(solution)/shard_map/all_gather | solution.py:262
  381.4 407.7 %copy-start.30 = (bf16[128,1024]{1,0:T(8,128)(2,1)S(1)}, bf16[128,1024]{1,0:T(8,128)(2,1)}, u32[]{:S(2)}) copy-start(bf16[128,1024]{1,0:T(8,128)(2,1)} %copy-done.29) | copy-start | bytes 786436
  765.2 12.1 collective-permute-start.15
  766.5 12.7 collective-permute-start.14
  769.4 5.9 collective-permute-start.16
  770.7 22.6 %collective-permute-start.13 = (bf16[40,1024]{1,0:T(8,128)(2,1)}, bf16[40,1024]{1,0:T(8,128)(2,1)}, u32[]{:S(2)}, u32[]{:S(2)}) collective-permute-start(bf16[40,1024]{1,0:T(8,128)(2,1)} %convert.58), channel_id=1, source_target_pairs={{0,10},{1,11},{2,12},{3,13},{4,14},{5,15},{6,16},{7,17},{8,18},{9,... | collective-permute-start | bytes 245768
  772.7 22.1 %collective-permute-start.12 = (bf16[40,1024]{1,0:T(8,128)(2,1)}, bf16[40,1024]{1,0:T(8,128)(2,1)}, u32[]{:S(2)}, u32[]{:S(2)}) collective-permute-start(bf16[40,1024]{1,0:T(8,128)(2,1)} %convert.58), channel_id=1, source_target_pairs={{0,9},{1,10},{2,11},{3,12},{4,13},{5,14},{6,15},{7,16},{8,17},{9,1... | collective-permute-start | bytes 245768
  775.4 21.3 %collective-permute-start.11 = (bf16[40,1024]{1,0:T(8,128)(2,1)}, bf16[40,1024]{1,0:T(8,128)(2,1)}, u32[]{:S(2)}, u32[]{:S(2)}) collective-permute-start(bf16[40,1024]{1,0:T(8,128)(2,1)} %convert.58), channel_id=1, source_target_pairs={{0,8},{1,9},{2,10},{3,11},{4,12},{5,13},{6,14},{7,15},{8,16},{9,17... | collective-permute-start | bytes 245768
  777.3 22.3 %collective-permute-start.10 = (bf16[40,1024]{1,0:T(8,128)(2,1)}, bf16[40,1024]{1,0:T(8,128)(2,1)}, u32[]{:S(2)}, u32[]{:S(2)}) collective-permute-start(bf16[40,1024]{1,0:T(8,128)(2,1)} %convert.58), channel_id=1, source_target_pairs={{0,7},{1,8},{2,9},{3,10},{4,11},{5,12},{6,13},{7,14},{8,15},{9,16}... | collective-permute-start | bytes 245768
  779.2 23.4 %collective-permute-start.9 = (bf16[40,1024]{1,0:T(8,128)(2,1)}, bf16[40,1024]{1,0:T(8,128)(2,1)}, u32[]{:S(2)}, u32[]{:S(2)}) collective-permute-start(bf16[40,1024]{1,0:T(8,128)(2,1)} %convert.58), channel_id=1, source_target_pairs={{0,6},{1,7},{2,8},{3,9},{4,10},{5,11},{6,12},{7,13},{8,14},{9,15},... | collective-permute-start | bytes 245768
  793.3 21.1 %collective-permute-start.8 = (bf16[40,1024]{1,0:T(8,128)(2,1)}, bf16[40,1024]{1,0:T(8,128)(2,1)S(1)}, u32[]{:S(2)}, u32[]{:S(2)}) collective-permute-start(bf16[40,1024]{1,0:T(8,128)(2,1)} %convert.58), channel_id=1, source_target_pairs={{0,5},{1,6},{2,7},{3,8},{4,9},{5,10},{6,11},{7,12},{8,13},{9,14},{... | collective-permute-start | bytes 245768
  794.7 19.7 %collective-permute-start.7 = (bf16[40,1024]{1,0:T(8,128)(2,1)}, bf16[40,1024]{1,0:T(8,128)(2,1)}, u32[]{:S(2)}, u32[]{:S(2)}) collective-permute-start(bf16[40,1024]{1,0:T(8,128)(2,1)} %convert.58), channel_id=1, source_target_pairs={{0,4},{1,5},{2,6},{3,7},{4,8},{5,9},{6,10},{7,11},{8,12},{9,13},{1... | collective-permute-start | bytes 245768
  796.7 17.8 collective-permute-start.6
  799.6 14.9 collective-permute-start.5
  802.7 11.8 collective-permute-start.4
  837.1 691.7 %reduce-scatter.10.cloned.1.call-start = ((), (), s32[]{:S(2)}) async-start(), calls=%async_computation.10 | async-start | bytes 4227072 | tf_op jit(solution)/shard_map/reduce_scatter | solution.py:234
  849.4 900.5 %reduce-scatter.8.cloned.1.call-start = ((), (), s32[]{:S(2)}) async-start(), calls=%async_computation.9 | async-start | bytes 12681216 | tf_op jit(solution)/shard_map/reduce_scatter | solution.py:232
  860.4 3.2 collective-permute-start.3
  862.1 3.7 collective-permute-start.2
  874.1 918.5 %all-gather.23.cloned.1.call-start = ((), (), s32[]{:S(2)}) async-start(), calls=%async_computation.12 | async-start | bytes 1253376 | tf_op jit(solution)/shard_map/all_gather | solution.py:256
  875.8 961.4 %all-gather.25.cloned.1.call-start = ((), (), s32[]{:S(2)}) async-start(), calls=%async_computation.14 | async-start | bytes 1253376 | tf_op jit(solution)/shard_map/all_gather | solution.py:259
  897.1 143.4 %copy-start.14 = (f32[128,1024]{1,0:T(8,128)S(1)}, f32[128,1024]{1,0:T(8,128)}, u32[]{:S(2)}) copy-start(f32[128,1024]{1,0:T(8,128)} %copy-done.12) | copy-start | bytes 1572868
  897.2 143.4 %copy-start.17 = (f32[128,1024]{1,0:T(8,128)S(1)}, f32[128,1024]{1,0:T(8,128)}, u32[]{:S(2)}) copy-start(f32[128,1024]{1,0:T(8,128)} %copy-done.15) | copy-start | bytes 1572868
  897.2 143.4 %copy-start.85 = (f32[128]{0:T(128)S(1)}, f32[128]{0:T(128)}, u32[]{:S(2)}) copy-start(f32[128]{0:T(128)} %get-tuple-element.92) | copy-start | bytes 1540
  897.2 143.4 %copy-start.86 = (f32[128]{0:T(128)S(1)}, f32[128]{0:T(128)}, u32[]{:S(2)}) copy-start(f32[128]{0:T(128)} %get-tuple-element.90) | copy-start | bytes 1540
  (80 other events, 559.2 us)
Sparse Core Ops, SparseCore 0:
  9.7 43.6 all-gather.12
  55.1 25.2 all-gather.14
  82.1 54.7 all-gather.16
  138.4 54.4 all-gather.18
  194.4 54.4 all-gather.20
  311.9 246.4 reduce-scatter.11
  564.6 247.2 reduce-scatter.13
  837.3 46.6 all-gather.26
  886.3 642.5 reduce-scatter.9
  1534.4 215.3 reduce-scatter.7
  1752.2 40.4 all-gather.22
  1794.9 42.3 all-gather.24
where the time goes:
time: 1860 us; the launch traced here: 1850 us
  waiting for transfers between devices  923 us (50%)
  blocking collectives  590 us (32%)
  matrix products  179 us (10%)
  local copies, waits for them, and re-layouts  70 us (4%)
  starting transfers between devices  41.1 us (2%)
  other arithmetic  27.1 us (1%)
    unnamed x3, blocking collectives  497 us
    reduce_scatter x1, waiting for transfers between devices, shards(): lax.psum_scatter(totals[3], ('dp', 'fsdp'), scatter_dimension=0, tiled=True)  483 us
    reduce_scatter x1, waiting for transfers between devices, shards(): lax.psum_scatter(totals[1], ('dp', 'fsdp'), scatter_dimension=0, tiled=True)  199 us
    all_gather x1, waiting for transfers between devices, shards(): lax.all_gather(params[5], 'fsdp', axis=0, tiled=True)  50.2 us
    all_gather x1, waiting for transfers between devices, shards(): lax.all_gather(params[6], 'fsdp', axis=0, tiled=True)  49.5 us
    all_gather x1, waiting for transfers between devices, shards(): lax.all_gather(params[7], 'fsdp', axis=0, tiled=True)  49.5 us
    all_gather x1, waiting for transfers between devices, shards(): lax.all_gather(shares[6].astype(jnp.bfloat16), 'dp', axis=0, tiled=True)  41.7 us
  transfers between devices with their start and end apart: 29, of which 11 were waited for; matrix products, arithmetic and copies ran while one was open for 32% of the time, Pallas kernels for 0%

commit v1 on v0

v1 whole, which is shorter than its diff:
```python
import jax
import jax.numpy as jnp
from jax import lax
from jax.sharding import Mesh, PartitionSpec as P

KW = 3
EPS = 1e-05
GROUP = ("z", "core")
EVERY = ("y", "x", "z", "core")
CONTRACT = (((0,), (0,)), ((), ()))
BACK_DIMS = (((1,), (1,)), ((), ()))
F32 = jnp.float32
BF16 = jnp.bfloat16


def dot(a, b, dims=(((1,), (0,)), ((), ()))):
    return lax.dot_general(a, b, dims, preferred_element_type=F32)


def shift(value, axis, distance):
    size = lax.axis_size(axis)
    return lax.ppermute(value, axis, [(i, (i + distance) % size) for i in range(size)])


def from_behind(block, distance):
    size = lax.axis_size(EVERY)
    route = [(i - distance, i) for i in range(size) if 0 <= i - distance < size]
    return lax.ppermute(block, EVERY, route)


def fetch(value, axis):
    return [value] + [shift(value, axis, d) for d in range(1, lax.axis_size(axis))]


def place(pieces, axis, dim, dtype):
    size = lax.axis_size(axis)
    here = lax.axis_index(axis)
    width = pieces[0].shape[dim]
    shape = list(pieces[0].shape)
    shape[dim] = width * size
    out = jnp.zeros(shape, dtype)
    for d, piece in enumerate(pieces):
        start = lax.rem(here - d + size, size) * width
        out = lax.dynamic_update_slice_in_dim(out, piece.astype(dtype), start, dim)
    return out


def gather(value, axis, dim, dtype=BF16):
    return place(fetch(value, axis), axis, dim, dtype)


def scatter_sum(value, axis, dim):
    size = lax.axis_size(axis)
    here = lax.axis_index(axis)
    width = value.shape[dim] // size

    def block(d):
        start = lax.rem(here + d, size) * width
        return lax.dynamic_slice_in_dim(value, start, width, dim)

    total = block(0).astype(F32)
    for d in range(1, size):
        total = total + shift(block(d).astype(BF16), axis, d).astype(F32)
    return total


def give_back(partial, axis):
    size = lax.axis_size(axis)
    rows = partial.shape[0] // size
    total = partial[:rows]
    for d in range(1, size):
        part = partial[d * rows : (d + 1) * rows].astype(BF16)
        total = total + shift(part, axis, -d).astype(F32)
    return total


def shards(
    block_input,
    seq_start,
    norm_gain,
    in_weight,
    conv_weight,
    out_weight,
    ffn_gain,
    gate_weight,
    up_weight,
    down_weight,
    cotangent,
):
    micro, rows, width = block_input.shape
    owned = norm_gain.shape[0]
    hidden_width = gate_weight.shape[1]
    n_x = lax.axis_size("x")
    n_group = lax.axis_size(GROUP)
    x_here = lax.axis_index("x")
    tokens = micro * rows

    grad_low = cotangent.reshape(tokens, width)
    grad_moved = jnp.concatenate(fetch(grad_low, "x"), 0)

    branch_weight = lax.all_gather(
        jnp.concatenate([in_weight, out_weight], 1), GROUP, axis=0, tiled=True
    )
    gains = lax.all_gather(
        jnp.concatenate(
            [norm_gain[None], ffn_gain[None], conv_weight, jnp.zeros((3, owned), BF16)], 0
        ),
        GROUP,
        axis=1,
        tiled=True,
    ).astype(F32)
    in_full = branch_weight[:, : 3 * width]
    out_full = branch_weight[:, 3 * width :]
    gain_one = gains[0]
    gain_two = gains[1]
    conv_taps = gains[2 : 2 + KW]

    piece = hidden_width // (n_group * n_x)
    share = piece * n_group

    def quarter(weight):
        split = weight.reshape(owned, n_group, n_x, piece)
        return lax.dynamic_index_in_dim(split, x_here, 2, False).reshape(owned, share)

    wide = lax.all_gather(
        jnp.concatenate([quarter(gate_weight), quarter(up_weight)], 1), GROUP, axis=0, tiled=True
    )
    down = lax.all_gather(
        lax.dynamic_slice_in_dim(down_weight, x_here * piece, piece, 0), GROUP, axis=0, tiled=True
    )

    inputs = block_input.reshape(tokens, width).astype(F32)
    inv_one = lax.rsqrt(jnp.mean(inputs * inputs, -1, keepdims=True) + EPS)
    normed_one = (inputs * inv_one * gain_one).astype(BF16)
    projected = dot(normed_one, in_full)
    b_part = projected[:, :width]
    c_part = projected[:, width : 2 * width]
    x_part = projected[:, 2 * width :]
    mixed = (b_part * x_part).reshape(micro, rows, width)
    rim = from_behind(mixed[:, rows - (KW - 1) :], 1)
    extended = jnp.concatenate([rim, mixed], 1)
    position = lax.axis_index(EVERY) * rows + lax.iota(jnp.int32, rows)
    masks = [(position[None] - k >= seq_start).astype(F32)[:, :, None] for k in range(KW)]
    conv_out = jnp.zeros_like(mixed)
    for k in range(KW):
        low = KW - 1 - k
        conv_out = conv_out + conv_taps[k] * extended[:, low : low + rows] * masks[k]
    conv_out = conv_out.reshape(tokens, width)
    gated = (c_part * conv_out).astype(BF16)
    resid = inputs + dot(gated, out_full)
    inv_two = lax.rsqrt(jnp.mean(resid * resid, -1, keepdims=True) + EPS)
    normed_two = (resid * inv_two * gain_two).astype(BF16)

    moved = jnp.concatenate(fetch(normed_two, "x"), 0)
    pre = dot(moved, wide)
    gate_pre = pre[:, :share]
    up_pre = pre[:, share:]
    sigma = jax.nn.sigmoid(gate_pre)
    hidden = (gate_pre * sigma * up_pre).astype(BF16)
    grad_hidden = dot(grad_moved, down, BACK_DIMS)
    grad_gate = (grad_hidden * up_pre * sigma * (1.0 + gate_pre * (1.0 - sigma))).astype(BF16)
    grad_up = (grad_hidden * gate_pre * sigma).astype(BF16)
    grad_wide = jnp.concatenate([grad_gate, grad_up], 1)
    grad_normed = give_back(dot(grad_wide, wide, BACK_DIMS), "x")
    result = (resid + give_back(dot(hidden, down), "x")).astype(BF16)
    wide_term = dot(moved, grad_wide, CONTRACT).astype(BF16)
    down_term = dot(hidden, grad_moved, CONTRACT).astype(BF16)
    wide_sum = lax.psum_scatter(wide_term, GROUP, scatter_dimension=0, tiled=True)
    down_sum = lax.psum_scatter(down_term, GROUP, scatter_dimension=0, tiled=True)

    grad_out = grad_low.astype(F32)
    ffn_term = jnp.sum(grad_normed * resid * inv_two, 0)
    hat_two = grad_normed * gain_two
    grad_resid = (
        grad_out
        + inv_two * hat_two
        - resid * inv_two**3 * jnp.mean(hat_two * resid, -1, keepdims=True)
    )
    grad_branch = grad_resid.astype(BF16)
    out_term = dot(gated, grad_branch, CONTRACT)
    grad_gated = dot(grad_branch, out_full, BACK_DIMS)
    grad_c = grad_gated * conv_out
    grad_conv = (grad_gated * c_part).reshape(micro, rows, width)
    tap_terms = []
    grad_extended = jnp.zeros_like(extended)
    for k in range(KW):
        low = KW - 1 - k
        masked = grad_conv * masks[k]
        tap_terms.append(jnp.sum(masked * extended[:, low : low + rows], (0, 1)))
        grad_extended = grad_extended + jnp.pad(
            masked * conv_taps[k], ((0, 0), (low, k), (0, 0))
        )
    incoming = from_behind(grad_extended[:, : KW - 1], -1)
    grad_mixed = grad_extended[:, KW - 1 :] + jnp.pad(
        incoming, ((0, 0), (rows - (KW - 1), 0), (0, 0))
    )
    grad_mixed = grad_mixed.reshape(tokens, width)
    grad_projected = jnp.concatenate([grad_mixed * x_part, grad_c, grad_mixed * b_part], 1).astype(
        BF16
    )
    in_term = dot(normed_one, grad_projected, CONTRACT)
    grad_first = dot(grad_projected, in_full, BACK_DIMS)
    norm_term = jnp.sum(grad_first * inputs * inv_one, 0)
    hat_one = grad_first * gain_one
    grad_input = (
        grad_resid
        + inv_one * hat_one
        - inputs * inv_one**3 * jnp.mean(hat_one * inputs, -1, keepdims=True)
    )

    small = jnp.pad(jnp.stack([norm_term, ffn_term] + tap_terms, 0), ((0, 123), (0, 0)))
    branch_term = jnp.concatenate(
        [in_term.astype(BF16), out_term.astype(BF16), small.T.astype(BF16)], 1
    )
    branch_sum = lax.psum_scatter(branch_term, GROUP, scatter_dimension=0, tiled=True)
    branch_sum = scatter_sum(scatter_sum(branch_sum, "y", 0), "x", 0).astype(BF16)
    branch_sum = gather(gather(branch_sum, "x", 0), "y", 0, F32)
    in_grad = branch_sum[:, : 3 * width]
    out_grad = branch_sum[:, 3 * width : 4 * width]
    gain_grads = branch_sum[:, 4 * width : 4 * width + 2 + KW].T

    wide_sum = gather(scatter_sum(wide_sum, "y", 0).astype(BF16), "y", 0)
    down_sum = gather(scatter_sum(down_sum, "y", 1).astype(BF16), "y", 1)
    wide_all = gather(wide_sum.reshape(1, owned, 2, n_group, piece), "x", 0)
    wide_all = wide_all.transpose(2, 1, 3, 0, 4).reshape(2, owned, hidden_width).astype(F32)
    down_grad = gather(down_sum, "x", 0, F32)
    return (
        result.reshape(micro, rows, width),
        grad_input.reshape(micro, rows, width),
        gain_grads[0],
        in_grad,
        gain_grads[2:],
        out_grad,
        gain_grads[1],
        wide_all[0],
        wide_all[1],
        down_grad,
    )


def solution(mesh):
    fine = Mesh(mesh.devices.reshape(4, 4, 4, 2), EVERY)
    token = P(None, EVERY, None)
    owner = P(GROUP, None)
    return jax.shard_map(
        shards,
        mesh=fine,
        in_specs=(
            token,
            P(None, EVERY),
            P(GROUP),
            owner,
            P(None, GROUP),
            owner,
            P(GROUP),
            owner,
            owner,
            owner,
            token,
        ),
        out_specs=(
            token,
            token,
            P(GROUP),
            owner,
            P(None, GROUP),
            owner,
            P(GROUP),
            owner,
            owner,
            owner,
        ),
        check_vma=False,
    )
```

time: 1860 us -> 406 us (0.22)
  waiting for transfers between devices: 923 us -> 170 us
  blocking collectives: 590 us -> 12.9 us
  matrix products: 179 us -> 64.4 us
  starting transfers between devices: 41.1 us -> 62.9 us
  local copies, waits for them, and re-layouts: 70 us -> 51.4 us
    reduce_scatter x4 -> x3, waiting for transfers between devices: 682 us -> 0.04 us  [the longest x1 0.02 us: shards(): lax.psum_scatter(down_term, GROUP, scatter_dimension=0, tiled=True)]
    unnamed x3 -> x0, blocking collectives: 497 us -> none
    all_gather x8 -> x3, waiting for transfers between devices: 235 us -> 37.8 us  [the longest x1 32.7 us: shards(): lax.all_gather(jnp.concatenate([in_weight, out_weight], 1), GROUP, axis=0...]
    ppermute x4 -> x44, waiting for transfers between devices: 1.96 us -> 132 us  [the longest x42 131 us: shift(): lax.ppermute(value, axis, [(i, (i + distance) % size) for i in range(size)])]
    dot_general x30 -> x12, matrix products: 179 us -> 64.4 us  [dot(): return lax.dot_general(a, b, dims, preferred_element_type=F32)]
    all_gather x6 -> x1, blocking collectives: 93.2 us -> 12.9 us  [shards(): lax.all_gather(jnp.concatenate([norm_gain[None], ffn_gain[None], conv_wei...]
    ppermute x4 -> x44, starting transfers between devices: 7.22 us -> 62.5 us  [the longest x42 58.9 us: shift(): lax.ppermute(value, axis, [(i, (i + distance) % size) for i in range(size)])]
    unnamed x13 -> x0, starting transfers between devices: 33.2 us -> none
  transfers between devices with their start and end apart: 29 -> 50, of which waited for: 11 -> 33; matrix products, arithmetic and copies ran while one was open for 32% -> 28% of each run, Pallas kernels for 0% -> 0%
where the time goes in v1:
time: 406 us; the launch traced here: 401 us
  waiting for transfers between devices  170 us (42%)
  matrix products  64.4 us (16%)
  starting transfers between devices  62.9 us (15%)
  local copies, waits for them, and re-layouts  51.4 us (13%)
  other arithmetic  23.7 us (6%)
  between operations  15.3 us (4%)
  blocking collectives  12.9 us (3%)
    ppermute x42, waiting for transfers between devices, shift(): lax.ppermute(value, axis, [(i, (i + distance) % size) for i in range(size)])  131 us
    dot_general x12, matrix products, dot(): return lax.dot_general(a, b, dims, preferred_element_type=F32)  64.4 us
    ppermute x42, starting transfers between devices, shift(): lax.ppermute(value, axis, [(i, (i + distance) % size) for i in range(size)])  58.9 us
    all_gather x1, waiting for transfers between devices, shards(): lax.all_gather(jnp.concatenate([in_weight, out_weight], 1), GROUP, axis=0...  32.7 us
    dynamic_update_slice x14, local copies, waits for them, and re-layouts, place(): out = lax.dynamic_update_slice_in_dim(out, piece.astype(dtype), start, dim)  21.8 us
    all_gather x1, blocking collectives, shards(): lax.all_gather(jnp.concatenate([norm_gain[None], ffn_gain[None], conv_wei...  12.9 us
    unnamed x57, local copies, waits for them, and re-layouts  12.2 us
  transfers between devices with their start and end apart: 50, of which 33 were waited for; matrix products, arithmetic and copies ran while one was open for 28% of the time, Pallas kernels for 0%

profile of v1, /device:TPU:0, one launch (start us, length us, event | category | flops | bytes accessed | tf_op | source)
XLA Modules:
  0.0 400.8 jit_solution(17795471604797769463)
XLA Ops:
  7.2 2.3 pad_maximum_fusion.8
  11.4 2.4 copy.42
  16.8 12.9 %all_gather.12 = bf16[8,1024]{1,0:T(8,128)(2,1)S(1)} all-gather(bf16[8,128]{1,0:T(8,128)(2,1)S(1)} %maximum_maximum_fusion), channel_id=1, replica_groups=mesh['y'=4,'x'=4,'z'=4,'core'=2] {'z','core'}, dimensions={1}, use_global_device_ids=true | all-gather | bytes 18432 | tf_op jit(solution)/shard_map/all_gather | solution.py:104
  30.1 32.7 %all-gather.4.cloned.1.call-done = bf16[1024,4096]{1,0:T(8,128)(2,1)} async-done(((bf16[128,4096]{1,0:T(8,128)(2,1)}), bf16[1024,4096]{1,0:T(8,128)(2,1)}) %all-gather.4.cloned.1.call-update) | async-done | bytes 8388624 | tf_op jit(solution)/shard_map/all_gather | solution.py:101
  62.8 4.6 %fusion.2 = f32[256,3072]{1,0:T(8,128)S(1)} fusion(bf16[256,1024]{1,0:T(8,128)(2,1)S(1)} %fusion.25, bf16[1024,4096]{1,0:T(8,128)(2,1)} %all-gather.4.cloned.1.call-done), kind=kOutput, calls=%fused_computation.5 | convolution fusion | flops 1610612736 | bytes 9961472 | tf_op jit(solution)/shard_map/dot_general | solution.py:17
  67.6 2.2 collective-permute-start
  71.6 2.4 multiply_reduce_fusion.5
  75.2 6.9 %collective-permute-start.3 = (bf16[256,1024]{1,0:T(8,128)(2,1)}, bf16[256,1024]{1,0:T(8,128)(2,1)}, u32[]{:S(2)}, u32[]{:S(2)}) collective-permute-start(bf16[256,1024]{1,0:T(8,128)(2,1)} %multiply_convert_fusion.3), channel_id=1, source_target_pairs={{0,24},{8,0},{16,8},{24,16},{1,25},{9,1},{17,9},{25,17},{2,26},{10... | collective-permute-start | bytes 1572872 | tf_op jit(solution)/shard_map/ppermute | solution.py:22
  83.8 2.4 collective-permute-start.9
  87.7 18.4 %collective-permute-done.3 = bf16[256,1024]{1,0:T(8,128)(2,1)} collective-permute-done((bf16[256,1024]{1,0:T(8,128)(2,1)}, bf16[256,1024]{1,0:T(8,128)(2,1)}, u32[]{:S(2)}, u32[]{:S(2)}) %collective-permute-start.3) | collective-permute-done | bytes 524320 | tf_op jit(solution)/shard_map/ppermute | solution.py:22
  106.8 3.2 collective-permute-done.1
  110.1 11.7 %fusion.32 = f32[1024,2304]{1,0:T(8,128)} fusion(bf16[1024,2304]{0,1:T(8,128)(2,1)} %all-gather.6.cloned.1.call-done, bf16[256,1024]{1,0:T(8,128)(2,1)} %collective-permute-done.3, bf16[256,1024]{1,0:T(8,128)(2,1)} %collective-permute-done.2, bf16[256,1024]{1,0:T(8,128)(2,1)} %collective-permute-done.1, bf16[256,1024]{1,0:T(8,128)(2,1)} %multiply_convert_fusion.3), kind=kOutput, calls=%fused_computation.88 | convolution fusion | flops 4840226816 | bytes 16252928 | tf_op jit(solution)/shard_map/dot_general | solution.py:17
  123.7 3.7 collective-permute-done.7
  127.4 5.1 %all-gather.8.cloned.1.call-done = bf16[1152,1024]{1,0:T(8,128)(2,1)} async-done(((bf16[144,1024]{1,0:T(8,128)(2,1)}), bf16[1152,1024]{1,0:T(8,128)(2,1)}) %all-gather.8.cloned.1.call-update) | async-done | bytes 2359312 | tf_op jit(solution)/shard_map/all_gather | solution.py:128
  132.5 10.3 %multiply_convert_fusion.1 = (bf16[1024,1152]{1,0:T(8,128)(2,1)}, bf16[1024,1152]{1,0:T(8,128)(2,1)}, bf16[1024,1152]{1,0:T(8,128)(2,1)S(1)}) fusion(f32[1024,2304]{1,0:T(8,128)} %fusion.32, bf16[1152,1024]{1,0:T(8,128)(2,1)} %all-gather.8.cloned.1.call-done, bf16[256,1024]{1,0:T(8,128)(2,1)} %collective-permute-done.9, ...), kind=kOutput, calls=%fused_computation.10 | convolution fusion | flops 2443182080 | bytes 20971520 | tf_op jit(solution)/shard_map/dot_general | solution.py:17
  144.3 5.6 %convolution_convert_fusion.2 = bf16[1152,1024]{1,0:T(8,128)(2,1)} fusion(bf16[1024,1152]{1,0:T(8,128)(2,1)S(1)} %get-tuple-element.57, bf16[256,1024]{1,0:T(8,128)(2,1)} %collective-permute-done.9, bf16[256,1024]{1,0:T(8,128)(2,1)} %collective-permute-done.8, bf16[256,1024]{1,0:T(8,128)(2,1)} %collective-permute-done.7, bf16[256,1024]{1,0:T(8,128)(2,1)} %bitcast.16), kind=kOutput, calls=%fused_computation.13 | convolution fusion | flops 2425487360 | bytes 6815744 | tf_op jit(solution)/shard_map/dot_general | solution.py:17
  150.1 10.4 %convolution_convert_fusion.1 = bf16[1024,2304]{1,0:T(8,128)(2,1)} fusion(bf16[1024,1152]{1,0:T(8,128)(2,1)} %get-tuple-element.56, bf16[1024,1152]{1,0:T(8,128)(2,1)} %get-tuple-element.55, bf16[256,1024]{1,0:T(8,128)(2,1)} %collective-permute-done.3, bf16[256,1024]{1,0:T(8,128)(2,1)} %collective-permute-done.2, ...), kind=kOutput, calls=%fused_computation.2 | convolution fusion | flops 4852023296 | bytes 11534336 | tf_op jit(solution)/shard_map/dot_general | solution.py:17
  160.6 8.4 %fusion.47 = (bf16[1024,1024]{1,0:T(8,128)(2,1)S(1)}, f32[1024,1024]{1,0:T(8,128)S(1)}) fusion(bf16[1024,2304]{0,1:T(8,128)(2,1)} %all-gather.6.cloned.1.call-done, bf16[1024,1152]{1,0:T(8,128)(2,1)} %get-tuple-element.56, bf16[1024,1152]{1,0:T(8,128)(2,1)} %get-tuple-element.55), kind=kOutput, calls=%fused_computation.147 | convolution fusion | flops 4842323968 | bytes 15728640 | tf_op jit(solution)/shard_map/dot_general | solution.py:17
  170.7 2.7 collective-permute-start.11
  174.9 2.9 fusion.48
  179.4 6.2 %collective-permute-done.12 = bf16[256,1024]{1,0:T(8,128)(2,1)S(1)} collective-permute-done((bf16[256,1024]{1,0:T(8,128)(2,1)S(1)}, bf16[256,1024]{1,0:T(8,128)(2,1)S(1)}, u32[]{:S(2)}, u32[]{:S(2)}) %collective-permute-start.12) | collective-permute-done | bytes 524320 | tf_op jit(solution)/shard_map/ppermute | solution.py:22
  186.9 10.5 %collective-permute-done.11 = bf16[256,1024]{1,0:T(8,128)(2,1)S(1)} collective-permute-done((bf16[256,1024]{1,0:T(8,128)(2,1)S(1)}, bf16[256,1024]{1,0:T(8,128)(2,1)S(1)}, u32[]{:S(2)}, u32[]{:S(2)}) %collective-permute-start.11) | collective-permute-done | bytes 524320 | tf_op jit(solution)/shard_map/ppermute | solution.py:22
  198.0 9.1 %collective-permute-done.6 = bf16[256,1024]{1,0:T(8,128)(2,1)S(1)} collective-permute-done((bf16[256,1024]{1,0:T(8,128)(2,1)S(1)}, bf16[256,1024]{1,0:T(8,128)(2,1)S(1)}, u32[]{:S(2)}, u32[]{:S(2)}) %collective-permute-start.6) | collective-permute-done | bytes 524320 | tf_op jit(solution)/shard_map/ppermute | solution.py:22
  207.1 12.2 %collective-permute-done.5 = bf16[256,1024]{1,0:T(8,128)(2,1)S(1)} collective-permute-done((bf16[256,1024]{1,0:T(8,128)(2,1)S(1)}, bf16[256,1024]{1,0:T(8,128)(2,1)S(1)}, u32[]{:S(2)}, u32[]{:S(2)}) %collective-permute-start.5) | collective-permute-done | bytes 524320 | tf_op jit(solution)/shard_map/ppermute | solution.py:22
  219.3 2.9 multiply_subtract_fusion
  228.2 2.9 fusion.30
  231.5 3.4 convolution_convert_fusion
  234.9 3.8 pad_maximum_fusion
  240.0 6.5 %collective-permute-start.37 = (bf16[144,256]{1,0:T(8,128)(2,1)S(1)}, bf16[144,256]{1,0:T(8,128)(2,1)S(1)}, u32[]{:S(2)}, u32[]{:S(2)}) collective-permute-start(bf16[144,256]{1,0:T(8,128)(2,1)S(1)} %get-tuple-element.84), channel_id=1, source_target_pairs={{0,96},{32,0},{64,32},{96,64},{1,97},{33,1},{65,33},{97,65},{2,98}... | collective-permute-start | bytes 221192 | tf_op jit(solution)/shard_map/ppermute | solution.py:22
  248.5 3.9 collective-permute-done.36
  264.6 2.9 collective-permute-start.42
  268.6 2.7 collective-permute-start.28
  273.9 2.1 collective-permute-done.28
  276.1 2.6 collective-permute-done.27
  281.8 2.1 collective-permute-start.30
  286.6 3.1 dynamic_update_slice.80
  292.2 5.1 %dynamic_update_slice.81 = bf16[128,2304]{0,1:T(8,128)(2,1)S(1)} dynamic-update-slice(bf16[128,2304]{0,1:T(8,128)(2,1)S(1)} %dynamic_update_slice.80, bf16[32,2304]{0,1:T(8,128)(2,1)S(1)} %copy.47, s32[]{:T(128)S(6)} %select_n.99, s32[]{:T(128)} %constant.108.clone.1) | dynamic-update-slice | bytes 294916 | tf_op jit(solution)/shard_map/dynamic_update_slice | solution.py:44
  298.6 5.1 %dynamic_update_slice.82 = bf16[128,2304]{0,1:T(8,128)(2,1)S(1)} dynamic-update-slice(bf16[128,2304]{0,1:T(8,128)(2,1)S(1)} %dynamic_update_slice.81, bf16[32,2304]{0,1:T(8,128)(2,1)S(1)} %copy.48, s32[]{:T(128)S(6)} %select_n.98, s32[]{:T(128)} %constant.108.clone.1) | dynamic-update-slice | bytes 294916 | tf_op jit(solution)/shard_map/dynamic_update_slice | solution.py:44
  305.0 5.1 %dynamic_update_slice.83 = bf16[128,2304]{0,1:T(8,128)(2,1)S(1)} dynamic-update-slice(bf16[128,2304]{0,1:T(8,128)(2,1)S(1)} %dynamic_update_slice.82, bf16[32,2304]{0,1:T(8,128)(2,1)S(1)} %copy.49, s32[]{:T(128)S(6)} %select_n.97, s32[]{:T(128)} %constant.108.clone.1) | dynamic-update-slice | bytes 294916 | tf_op jit(solution)/shard_map/dynamic_update_slice | solution.py:44
  313.1 2.6 collective-permute-start.34
  316.2 22.2 %collective-permute-done.32 = bf16[1,128,2,8,144]{1,4,3,2,0:T(8,128)(2,1)S(1)} collective-permute-done((bf16[1,128,2,8,144]{1,4,3,2,0:T(8,128)(2,1)S(1)}, bf16[1,128,2,8,144]{1,4,3,2,0:T(8,128)(2,1)S(1)}, u32[]{:S(2)}, u32[]{:S(2)}) %collective-permute-start.32) | collective-permute-done | bytes 589856 | tf_op jit(solution)/shard_map/ppermute | solution.py:22
  343.1 6.1 %collective-permute-done.16 = bf16[32,4224]{1,0:T(8,128)(2,1)S(1)} collective-permute-done((bf16[32,4224]{1,0:T(8,128)(2,1)S(1)}, bf16[32,4224]{1,0:T(8,128)(2,1)S(1)}, u32[]{:S(2)}, u32[]{:S(2)}) %collective-permute-start.16) | collective-permute-done | bytes 270368 | tf_op jit(solution)/shard_map/ppermute | solution.py:22
  350.9 3.0 collective-permute-done.14
  365.0 3.0 copy.55
  370.0 2.6 collective-permute-start.21
  372.9 2.9 collective-permute-done.21
  377.0 3.0 collective-permute-start.24
  380.4 9.0 %collective-permute-done.23 = bf16[32,4224]{1,0:T(8,128)(2,1)S(1)} collective-permute-done((bf16[32,4224]{1,0:T(8,128)(2,1)S(1)}, bf16[32,4224]{1,0:T(8,128)(2,1)S(1)}, u32[]{:S(2)}, u32[]{:S(2)}) %collective-permute-start.23) | collective-permute-done | bytes 270368 | tf_op jit(solution)/shard_map/ppermute | solution.py:22
  (218 shorter events, 87.6 us)
Async XLA Ops:
  7.2 55.6 %all-gather.4.cloned.1.call-start = ((), (), s32[]{:S(2)}) async-start(), calls=%async_computation.3 | async-start | bytes 9437184 | tf_op jit(solution)/shard_map/all_gather | solution.py:101
  9.6 97.2 %all-gather.6.cloned.1.call-start = ((), (), s32[]{:S(2)}) async-start(), calls=%async_computation.4 | async-start | bytes 5308416 | tf_op jit(solution)/shard_map/all_gather | solution.py:125
  15.7 116.8 %all-gather.8.cloned.1.call-start = ((), (), s32[]{:S(2)}) async-start(), calls=%async_computation.5 | async-start | bytes 2654208 | tf_op jit(solution)/shard_map/all_gather | solution.py:128
  16.5 222.4 %reduce-scatter.8.cloned.1.call-start = ((), (), s32[]{:S(2)}) async-start(), calls=%async_computation.8 | async-start | bytes 2654208 | tf_op jit(solution)/shard_map/reduce_scatter | solution.py:169
  75.2 30.9 %collective-permute-start.3 = (bf16[256,1024]{1,0:T(8,128)(2,1)}, bf16[256,1024]{1,0:T(8,128)(2,1)}, u32[]{:S(2)}, u32[]{:S(2)}) collective-permute-start(bf16[256,1024]{1,0:T(8,128)(2,1)} %multiply_convert_fusion.3), channel_id=1, source_target_pairs={{0,24},{8,0},{16,8},{24,16},{1,25},{9,1},{17,9},{25,17},{2,26},{10... | collective-permute-start | bytes 1572872 | tf_op jit(solution)/shard_map/ppermute | solution.py:22
  82.1 24.7 %collective-permute-start.2 = (bf16[256,1024]{1,0:T(8,128)(2,1)}, bf16[256,1024]{1,0:T(8,128)(2,1)}, u32[]{:S(2)}, u32[]{:S(2)}) collective-permute-start(bf16[256,1024]{1,0:T(8,128)(2,1)} %multiply_convert_fusion.3), channel_id=1, source_target_pairs={{0,16},{8,24},{16,0},{24,8},{1,17},{9,25},{17,1},{25,9},{2,18},{10... | collective-permute-start | bytes 1572872 | tf_op jit(solution)/shard_map/ppermute | solution.py:22
  82.9 27.1 %collective-permute-start.1 = (bf16[256,1024]{1,0:T(8,128)(2,1)}, bf16[256,1024]{1,0:T(8,128)(2,1)}, u32[]{:S(2)}, u32[]{:S(2)}) collective-permute-start(bf16[256,1024]{1,0:T(8,128)(2,1)} %multiply_convert_fusion.3), channel_id=1, source_target_pairs={{0,8},{8,16},{16,24},{24,0},{1,9},{9,17},{17,25},{25,1},{2,10},{10... | collective-permute-start | bytes 1572872 | tf_op jit(solution)/shard_map/ppermute | solution.py:22
  83.8 39.9 %collective-permute-start.9 = (bf16[256,1024]{1,0:T(8,128)(2,1)}, bf16[256,1024]{1,0:T(8,128)(2,1)}, u32[]{:S(2)}, u32[]{:S(2)}) collective-permute-start(bf16[256,1024]{1,0:T(8,128)(2,1)} %bitcast.16), channel_id=1, source_target_pairs={{0,24},{8,0},{16,8},{24,16},{1,25},{9,1},{17,9},{25,17},{2,26},{10... | collective-permute-start | bytes 1572872 | tf_op jit(solution)/shard_map/ppermute | solution.py:22
  86.2 37.6 %collective-permute-start.8 = (bf16[256,1024]{1,0:T(8,128)(2,1)}, bf16[256,1024]{1,0:T(8,128)(2,1)}, u32[]{:S(2)}, u32[]{:S(2)}) collective-permute-start(bf16[256,1024]{1,0:T(8,128)(2,1)} %bitcast.16), channel_id=1, source_target_pairs={{0,16},{8,24},{16,0},{24,8},{1,17},{9,25},{17,1},{25,9},{2,18},{10... | collective-permute-start | bytes 1572872 | tf_op jit(solution)/shard_map/ppermute | solution.py:22
  106.0 21.4 %collective-permute-start.7 = (bf16[256,1024]{1,0:T(8,128)(2,1)}, bf16[256,1024]{1,0:T(8,128)(2,1)}, u32[]{:S(2)}, u32[]{:S(2)}) collective-permute-start(bf16[256,1024]{1,0:T(8,128)(2,1)} %bitcast.16), channel_id=1, source_target_pairs={{0,8},{8,16},{16,24},{24,0},{1,9},{9,17},{17,25},{25,1},{2,10},{10... | collective-permute-start | bytes 1572872 | tf_op jit(solution)/shard_map/ppermute | solution.py:22
  149.9 117.7 %reduce-scatter.6.cloned.1.call-start = ((), (), s32[]{:S(2)}) async-start(), calls=%async_computation.7 | async-start | bytes 5308416 | tf_op jit(solution)/shard_map/reduce_scatter | solution.py:168
  160.5 178.0 %reduce-scatter.4.cloned.1.call-start = ((), (), s32[]{:S(2)}) async-start(), calls=%async_computation.6 | async-start | bytes 9732096 | tf_op jit(solution)/shard_map/reduce_scatter | solution.py:215
  169.2 16.4 %collective-permute-start.12 = (bf16[256,1024]{1,0:T(8,128)(2,1)S(1)}, bf16[256,1024]{1,0:T(8,128)(2,1)S(1)}, u32[]{:S(2)}, u32[]{:S(2)}) collective-permute-start(bf16[256,1024]{1,0:T(8,128)(2,1)S(1)} %get-tuple-element.63), channel_id=1, source_target_pairs={{0,8},{8,16},{16,24},{24,0},{1,9},{9,17},{17,25},{25,1},{2,10},{10... | collective-permute-start | bytes 1572872 | tf_op jit(solution)/shard_map/ppermute | solution.py:22
  170.7 26.7 %collective-permute-start.11 = (bf16[256,1024]{1,0:T(8,128)(2,1)S(1)}, bf16[256,1024]{1,0:T(8,128)(2,1)S(1)}, u32[]{:S(2)}, u32[]{:S(2)}) collective-permute-start(bf16[256,1024]{1,0:T(8,128)(2,1)S(1)} %get-tuple-element.64), channel_id=1, source_target_pairs={{0,16},{8,24},{16,0},{24,8},{1,17},{9,25},{17,1},{25,9},{2,18},{10... | collective-permute-start | bytes 1572872 | tf_op jit(solution)/shard_map/ppermute | solution.py:22
  173.4 24.0 %collective-permute-start.10 = (bf16[256,1024]{1,0:T(8,128)(2,1)S(1)}, bf16[256,1024]{1,0:T(8,128)(2,1)S(1)}, u32[]{:S(2)}, u32[]{:S(2)}) collective-permute-start(bf16[256,1024]{1,0:T(8,128)(2,1)S(1)} %get-tuple-element.62), channel_id=1, source_target_pairs={{0,24},{8,0},{16,8},{24,16},{1,25},{9,1},{17,9},{25,17},{2,26},{10... | collective-permute-start | bytes 1572872 | tf_op jit(solution)/shard_map/ppermute | solution.py:22
  177.9 29.2 %collective-permute-start.6 = (bf16[256,1024]{1,0:T(8,128)(2,1)S(1)}, bf16[256,1024]{1,0:T(8,128)(2,1)S(1)}, u32[]{:S(2)}, u32[]{:S(2)}) collective-permute-start(bf16[256,1024]{1,0:T(8,128)(2,1)S(1)} %get-tuple-element.66), channel_id=1, source_target_pairs={{0,8},{8,16},{16,24},{24,0},{1,9},{9,17},{17,25},{25,1},{2,10},{10... | collective-permute-start | bytes 1572872 | tf_op jit(solution)/shard_map/ppermute | solution.py:22
  178.5 40.7 %collective-permute-start.5 = (bf16[256,1024]{1,0:T(8,128)(2,1)S(1)}, bf16[256,1024]{1,0:T(8,128)(2,1)S(1)}, u32[]{:S(2)}, u32[]{:S(2)}) collective-permute-start(bf16[256,1024]{1,0:T(8,128)(2,1)S(1)} %get-tuple-element.67), channel_id=1, source_target_pairs={{0,16},{8,24},{16,0},{24,8},{1,17},{9,25},{17,1},{25,9},{2,18},{10... | collective-permute-start | bytes 1572872 | tf_op jit(solution)/shard_map/ppermute | solution.py:22
  185.6 33.7 %collective-permute-start.4 = (bf16[256,1024]{1,0:T(8,128)(2,1)S(1)}, bf16[256,1024]{1,0:T(8,128)(2,1)S(1)}, u32[]{:S(2)}, u32[]{:S(2)}) collective-permute-start(bf16[256,1024]{1,0:T(8,128)(2,1)S(1)} %get-tuple-element.65), channel_id=1, source_target_pairs={{0,24},{8,0},{16,8},{24,16},{1,25},{9,1},{17,9},{25,17},{2,26},{10... | collective-permute-start | bytes 1572872 | tf_op jit(solution)/shard_map/ppermute | solution.py:22
  240.0 8.5 %collective-permute-start.37 = (bf16[144,256]{1,0:T(8,128)(2,1)S(1)}, bf16[144,256]{1,0:T(8,128)(2,1)S(1)}, u32[]{:S(2)}, u32[]{:S(2)}) collective-permute-start(bf16[144,256]{1,0:T(8,128)(2,1)S(1)} %get-tuple-element.84), channel_id=1, source_target_pairs={{0,96},{32,0},{64,32},{96,64},{1,97},{33,1},{65,33},{97,65},{2,98}... | collective-permute-start | bytes 221192 | tf_op jit(solution)/shard_map/ppermute | solution.py:22
  246.5 5.9 %collective-permute-start.36 = (bf16[144,256]{1,0:T(8,128)(2,1)S(1)}, bf16[144,256]{1,0:T(8,128)(2,1)S(1)}, u32[]{:S(2)}, u32[]{:S(2)}) collective-permute-start(bf16[144,256]{1,0:T(8,128)(2,1)S(1)} %get-tuple-element.85), channel_id=1, source_target_pairs={{0,64},{32,96},{64,0},{96,32},{1,65},{33,97},{65,1},{97,33},{2,66}... | collective-permute-start | bytes 221192 | tf_op jit(solution)/shard_map/ppermute | solution.py:22
  247.0 6.1 %collective-permute-start.35 = (bf16[144,256]{1,0:T(8,128)(2,1)S(1)}, bf16[144,256]{1,0:T(8,128)(2,1)S(1)}, u32[]{:S(2)}, u32[]{:S(2)}) collective-permute-start(bf16[144,256]{1,0:T(8,128)(2,1)S(1)} %get-tuple-element.83), channel_id=1, source_target_pairs={{0,32},{32,64},{64,96},{96,0},{1,33},{33,65},{65,97},{97,1},{2,34}... | collective-permute-start | bytes 221192 | tf_op jit(solution)/shard_map/ppermute | solution.py:22
  255.5 5.6 %collective-permute-start.38 = (bf16[144,256]{1,0:T(8,128)(2,1)S(1)}, bf16[144,256]{1,0:T(8,128)(2,1)S(1)}, u32[]{:S(2)}, u32[]{:S(2)}) collective-permute-start(bf16[144,256]{1,0:T(8,128)(2,1)S(1)} %get-tuple-element.49), channel_id=1, source_target_pairs={{0,32},{32,64},{64,96},{96,0},{1,33},{33,65},{65,97},{97,1},{2,34}... | collective-permute-start | bytes 221192 | tf_op jit(solution)/shard_map/ppermute | solution.py:22
  256.8 5.9 %collective-permute-start.39 = (bf16[144,256]{1,0:T(8,128)(2,1)S(1)}, bf16[144,256]{1,0:T(8,128)(2,1)S(1)}, u32[]{:S(2)}, u32[]{:S(2)}) collective-permute-start(bf16[144,256]{1,0:T(8,128)(2,1)S(1)} %get-tuple-element.49), channel_id=1, source_target_pairs={{0,64},{32,96},{64,0},{96,32},{1,65},{33,97},{65,1},{97,33},{2,66}... | collective-permute-start | bytes 221192 | tf_op jit(solution)/shard_map/ppermute | solution.py:22
  258.8 5.2 %collective-permute-start.40 = (bf16[144,256]{1,0:T(8,128)(2,1)S(1)}, bf16[144,256]{1,0:T(8,128)(2,1)S(1)}, u32[]{:S(2)}, u32[]{:S(2)}) collective-permute-start(bf16[144,256]{1,0:T(8,128)(2,1)S(1)} %get-tuple-element.49), channel_id=1, source_target_pairs={{0,96},{32,0},{64,32},{96,64},{1,97},{33,1},{65,33},{97,65},{2,98}... | collective-permute-start | bytes 221192 | tf_op jit(solution)/shard_map/ppermute | solution.py:22
  264.6 19.2 %collective-permute-start.41 = (bf16[144,1024]{1,0:T(8,128)(2,1)}, bf16[144,1024]{1,0:T(8,128)(2,1)S(1)}, u32[]{:S(2)}, u32[]{:S(2)}) collective-permute-start(bf16[144,1024]{1,0:T(8,128)(2,1)} %constant_dynamic-update-slice_fusion), channel_id=1, source_target_pairs={{0,8},{8,16},{16,24},{24,0},{1,9},{9,17},{17,25},{25,1},{2,10},{10... | collective-permute-start | bytes 884744 | tf_op jit(solution)/shard_map/ppermute | solution.py:22
  264.6 45.7 %collective-permute-start.42 = (bf16[144,1024]{1,0:T(8,128)(2,1)}, bf16[144,1024]{1,0:T(8,128)(2,1)}, u32[]{:S(2)}, u32[]{:S(2)}) collective-permute-start(bf16[144,1024]{1,0:T(8,128)(2,1)} %constant_dynamic-update-slice_fusion), channel_id=1, source_target_pairs={{0,16},{8,24},{16,0},{24,8},{1,17},{9,25},{17,1},{25,9},{2,18},{10... | collective-permute-start | bytes 884744 | tf_op jit(solution)/shard_map/ppermute | solution.py:22
  268.6 7.4 %collective-permute-start.28 = (bf16[32,2304]{1,0:T(8,128)(2,1)S(1)}, bf16[32,2304]{1,0:T(8,128)(2,1)S(1)}, u32[]{:S(2)}, u32[]{:S(2)}) collective-permute-start(bf16[32,2304]{1,0:T(8,128)(2,1)S(1)} %get-tuple-element.78), channel_id=1, source_target_pairs={{0,96},{32,0},{64,32},{96,64},{1,97},{33,1},{65,33},{97,65},{2,98}... | collective-permute-start | bytes 442376 | tf_op jit(solution)/shard_map/ppermute | solution.py:22
  271.3 7.4 %collective-permute-start.27 = (bf16[32,2304]{1,0:T(8,128)(2,1)S(1)}, bf16[32,2304]{1,0:T(8,128)(2,1)S(1)}, u32[]{:S(2)}, u32[]{:S(2)}) collective-permute-start(bf16[32,2304]{1,0:T(8,128)(2,1)S(1)} %get-tuple-element.79), channel_id=1, source_target_pairs={{0,64},{32,96},{64,0},{96,32},{1,65},{33,97},{65,1},{97,33},{2,66}... | collective-permute-start | bytes 442376 | tf_op jit(solution)/shard_map/ppermute | solution.py:22
  272.0 8.1 %collective-permute-start.26 = (bf16[32,2304]{1,0:T(8,128)(2,1)S(1)}, bf16[32,2304]{1,0:T(8,128)(2,1)S(1)}, u32[]{:S(2)}, u32[]{:S(2)}) collective-permute-start(bf16[32,2304]{1,0:T(8,128)(2,1)S(1)} %get-tuple-element.77), channel_id=1, source_target_pairs={{0,32},{32,64},{64,96},{96,0},{1,33},{33,65},{65,97},{97,1},{2,34}... | collective-permute-start | bytes 442376 | tf_op jit(solution)/shard_map/ppermute | solution.py:22
  276.1 35.3 %collective-permute-start.43 = (bf16[144,1024]{1,0:T(8,128)(2,1)}, bf16[144,1024]{1,0:T(8,128)(2,1)}, u32[]{:S(2)}, u32[]{:S(2)}) collective-permute-start(bf16[144,1024]{1,0:T(8,128)(2,1)} %constant_dynamic-update-slice_fusion), channel_id=1, source_target_pairs={{0,24},{8,0},{16,8},{24,16},{1,25},{9,1},{17,9},{25,17},{2,26},{10... | collective-permute-start | bytes 884744 | tf_op jit(solution)/shard_map/ppermute | solution.py:22
  281.8 9.2 %collective-permute-start.29 = (bf16[32,2304]{1,0:T(8,128)(2,1)}, bf16[32,2304]{1,0:T(8,128)(2,1)}, u32[]{:S(2)}, u32[]{:S(2)}) collective-permute-start(bf16[32,2304]{1,0:T(8,128)(2,1)} %add_convert_fusion), channel_id=1, source_target_pairs={{0,32},{32,64},{64,96},{96,0},{1,33},{33,65},{65,97},{97,1},{2,34}... | collective-permute-start | bytes 442376 | tf_op jit(solution)/shard_map/ppermute | solution.py:22
  281.8 15.6 %collective-permute-start.30 = (bf16[32,2304]{1,0:T(8,128)(2,1)}, bf16[32,2304]{1,0:T(8,128)(2,1)}, u32[]{:S(2)}, u32[]{:S(2)}) collective-permute-start(bf16[32,2304]{1,0:T(8,128)(2,1)} %add_convert_fusion), channel_id=1, source_target_pairs={{0,64},{32,96},{64,0},{96,32},{1,65},{33,97},{65,1},{97,33},{2,66}... | collective-permute-start | bytes 442376 | tf_op jit(solution)/shard_map/ppermute | solution.py:22
  283.8 19.9 %collective-permute-start.31 = (bf16[32,2304]{1,0:T(8,128)(2,1)}, bf16[32,2304]{1,0:T(8,128)(2,1)}, u32[]{:S(2)}, u32[]{:S(2)}) collective-permute-start(bf16[32,2304]{1,0:T(8,128)(2,1)} %add_convert_fusion), channel_id=1, source_target_pairs={{0,96},{32,0},{64,32},{96,64},{1,97},{33,1},{65,33},{97,65},{2,98}... | collective-permute-start | bytes 442376 | tf_op jit(solution)/shard_map/ppermute | solution.py:22
  310.2 28.3 %collective-permute-start.32 = (bf16[1,128,2,8,144]{1,4,3,2,0:T(8,128)(2,1)S(1)}, bf16[1,128,2,8,144]{1,4,3,2,0:T(8,128)(2,1)S(1)}, u32[]{:S(2)}, u32[]{:S(2)}) collective-permute-start(bf16[1,128,2,8,144]{1,4,3,2,0:T(8,128)(2,1)S(1)} %bitcast.91), channel_id=1, source_target_pairs={{0,8},{8,16},{16,24},{24,0},{1,9},{9,17},{17,25},{25,1},{2,10},{10... | collective-permute-start | bytes 1769480 | tf_op jit(solution)/shard_map/ppermute | solution.py:22
  312.4 29.5 %collective-permute-start.33 = (bf16[1,128,2,8,144]{1,4,3,2,0:T(8,128)(2,1)S(1)}, bf16[1,128,2,8,144]{1,4,3,2,0:T(8,128)(2,1)}, u32[]{:S(2)}, u32[]{:S(2)}) collective-permute-start(bf16[1,128,2,8,144]{1,4,3,2,0:T(8,128)(2,1)S(1)} %bitcast.92), channel_id=1, source_target_pairs={{0,16},{8,24},{16,0},{24,8},{1,17},{9,25},{17,1},{25,9},{2,18},{10... | collective-permute-start | bytes 1769480 | tf_op jit(solution)/shard_map/ppermute | solution.py:22
  313.1 29.9 %collective-permute-start.34 = (bf16[1,128,2,8,144]{1,4,3,2,0:T(8,128)(2,1)S(1)}, bf16[1,128,2,8,144]{1,4,3,2,0:T(8,128)(2,1)S(1)}, u32[]{:S(2)}, u32[]{:S(2)}) collective-permute-start(bf16[1,128,2,8,144]{1,4,3,2,0:T(8,128)(2,1)S(1)} %bitcast.93), channel_id=1, source_target_pairs={{0,24},{8,0},{16,8},{24,16},{1,25},{9,1},{17,9},{25,17},{2,26},{10... | collective-permute-start | bytes 1769480 | tf_op jit(solution)/shard_map/ppermute | solution.py:22
  339.8 9.5 %collective-permute-start.16 = (bf16[32,4224]{1,0:T(8,128)(2,1)S(1)}, bf16[32,4224]{1,0:T(8,128)(2,1)S(1)}, u32[]{:S(2)}, u32[]{:S(2)}) collective-permute-start(bf16[32,4224]{1,0:T(8,128)(2,1)S(1)} %get-tuple-element.69), channel_id=1, source_target_pairs={{0,96},{32,0},{64,32},{96,64},{1,97},{33,1},{65,33},{97,65},{2,98}... | collective-permute-start | bytes 811016 | tf_op jit(solution)/shard_map/ppermute | solution.py:22
  339.8 11.0 %collective-permute-start.15 = (bf16[32,4224]{1,0:T(8,128)(2,1)S(1)}, bf16[32,4224]{1,0:T(8,128)(2,1)S(1)}, u32[]{:S(2)}, u32[]{:S(2)}) collective-permute-start(bf16[32,4224]{1,0:T(8,128)(2,1)S(1)} %get-tuple-element.70), channel_id=1, source_target_pairs={{0,64},{32,96},{64,0},{96,32},{1,65},{33,97},{65,1},{97,33},{2,66}... | collective-permute-start | bytes 811016 | tf_op jit(solution)/shard_map/ppermute | solution.py:22
  340.3 13.5 %collective-permute-start.14 = (bf16[32,4224]{1,0:T(8,128)(2,1)S(1)}, bf16[32,4224]{1,0:T(8,128)(2,1)S(1)}, u32[]{:S(2)}, u32[]{:S(2)}) collective-permute-start(bf16[32,4224]{1,0:T(8,128)(2,1)S(1)} %get-tuple-element.68), channel_id=1, source_target_pairs={{0,32},{32,64},{64,96},{96,0},{1,33},{33,65},{65,97},{97,1},{2,34}... | collective-permute-start | bytes 811016 | tf_op jit(solution)/shard_map/ppermute | solution.py:22
  355.0 4.5 %collective-permute-start.19 = (bf16[8,4224]{1,0:T(8,128)(2,1)S(1)}, bf16[8,4224]{1,0:T(8,128)(2,1)S(1)}, u32[]{:S(2)}, u32[]{:S(2)}) collective-permute-start(bf16[8,4224]{1,0:T(8,128)(2,1)S(1)} %get-tuple-element.81), channel_id=1, source_target_pairs={{0,24},{8,0},{16,8},{24,16},{1,25},{9,1},{17,9},{25,17},{2,26},{10... | collective-permute-start | bytes 202760 | tf_op jit(solution)/shard_map/ppermute | solution.py:22
  355.0 6.0 %collective-permute-start.18 = (bf16[8,4224]{1,0:T(8,128)(2,1)S(1)}, bf16[8,4224]{1,0:T(8,128)(2,1)S(1)}, u32[]{:S(2)}, u32[]{:S(2)}) collective-permute-start(bf16[8,4224]{1,0:T(8,128)(2,1)S(1)} %get-tuple-element.82), channel_id=1, source_target_pairs={{0,16},{8,24},{16,0},{24,8},{1,17},{9,25},{17,1},{25,9},{2,18},{10... | collective-permute-start | bytes 202760 | tf_op jit(solution)/shard_map/ppermute | solution.py:22
  355.1 6.9 %collective-permute-start.17 = (bf16[8,4224]{1,0:T(8,128)(2,1)S(1)}, bf16[8,4224]{1,0:T(8,128)(2,1)S(1)}, u32[]{:S(2)}, u32[]{:S(2)}) collective-permute-start(bf16[8,4224]{1,0:T(8,128)(2,1)S(1)} %get-tuple-element.80), channel_id=1, source_target_pairs={{0,8},{8,16},{16,24},{24,0},{1,9},{9,17},{17,25},{25,1},{2,10},{10... | collective-permute-start | bytes 202760 | tf_op jit(solution)/shard_map/ppermute | solution.py:22
  362.1 10.8 %collective-permute-start.20 = (bf16[8,4224]{1,0:T(8,128)(2,1)S(1)}, bf16[8,4224]{1,0:T(8,128)(2,1)S(1)}, u32[]{:S(2)}, u32[]{:S(2)}) collective-permute-start(bf16[8,4224]{1,0:T(8,128)(2,1)S(1)} %get-tuple-element.51), channel_id=1, source_target_pairs={{0,8},{8,16},{16,24},{24,0},{1,9},{9,17},{17,25},{25,1},{2,10},{10... | collective-permute-start | bytes 202760 | tf_op jit(solution)/shard_map/ppermute | solution.py:22
  370.0 5.8 %collective-permute-start.21 = (bf16[8,4224]{1,0:T(8,128)(2,1)S(1)}, bf16[8,4224]{1,0:T(8,128)(2,1)S(1)}, u32[]{:S(2)}, u32[]{:S(2)}) collective-permute-start(bf16[8,4224]{1,0:T(8,128)(2,1)S(1)} %get-tuple-element.51), channel_id=1, source_target_pairs={{0,16},{8,24},{16,0},{24,8},{1,17},{9,25},{17,1},{25,9},{2,18},{10... | collective-permute-start | bytes 202760 | tf_op jit(solution)/shard_map/ppermute | solution.py:22
  372.6 4.3 %collective-permute-start.22 = (bf16[8,4224]{1,0:T(8,128)(2,1)S(1)}, bf16[8,4224]{1,0:T(8,128)(2,1)S(1)}, u32[]{:S(2)}, u32[]{:S(2)}) collective-permute-start(bf16[8,4224]{1,0:T(8,128)(2,1)S(1)} %get-tuple-element.51), channel_id=1, source_target_pairs={{0,24},{8,0},{16,8},{24,16},{1,25},{9,1},{17,9},{25,17},{2,26},{10... | collective-permute-start | bytes 202760 | tf_op jit(solution)/shard_map/ppermute | solution.py:22
  376.9 12.5 %collective-permute-start.23 = (bf16[32,4224]{1,0:T(8,128)(2,1)S(1)}, bf16[32,4224]{1,0:T(8,128)(2,1)S(1)}, u32[]{:S(2)}, u32[]{:S(2)}) collective-permute-start(bf16[32,4224]{1,0:T(8,128)(2,1)S(1)} %constant_dynamic-update-slice_fusion.5), channel_id=1, source_target_pairs={{0,32},{32,64},{64,96},{96,0},{1,33},{33,65},{65,97},{97,1},{2,34}... | collective-permute-start | bytes 811016 | tf_op jit(solution)/shard_map/ppermute | solution.py:22
  377.0 12.5 %collective-permute-start.24 = (bf16[32,4224]{1,0:T(8,128)(2,1)S(1)}, bf16[32,4224]{1,0:T(8,128)(2,1)S(1)}, u32[]{:S(2)}, u32[]{:S(2)}) collective-permute-start(bf16[32,4224]{1,0:T(8,128)(2,1)S(1)} %constant_dynamic-update-slice_fusion.5), channel_id=1, source_target_pairs={{0,64},{32,96},{64,0},{96,32},{1,65},{33,97},{65,1},{97,33},{2,66}... | collective-permute-start | bytes 811016 | tf_op jit(solution)/shard_map/ppermute | solution.py:22
  380.0 10.1 %collective-permute-start.25 = (bf16[32,4224]{1,0:T(8,128)(2,1)S(1)}, bf16[32,4224]{1,0:T(8,128)(2,1)S(1)}, u32[]{:S(2)}, u32[]{:S(2)}) collective-permute-start(bf16[32,4224]{1,0:T(8,128)(2,1)S(1)} %constant_dynamic-update-slice_fusion.5), channel_id=1, source_target_pairs={{0,96},{32,0},{64,32},{96,64},{1,97},{33,1},{65,33},{97,65},{2,98}... | collective-permute-start | bytes 811016 | tf_op jit(solution)/shard_map/ppermute | solution.py:22
  (28 other events, 391.2 us)
Sparse Core Ops, SparseCore 0:
  10.3 52.4 all-gather.3
  65.0 38.4 all-gather.5
  105.8 26.6 all-gather.7
  150.0 35.0 reduce-scatter.7
  187.4 38.0 reduce-scatter.5
  238.8 58.9 reduce-scatter.3
